TPU v7x, 32 devices: a whole 2x2x4 slice. The times are simulated.
32 devices in a mesh: groups: 2 (over y), section: 4 (over z), fsdp: 4 (over x, core).
Axes of the slice: x: 2, y: 2, z: 4, core: 2. Of those that a mesh axis runs over, the one named last changes fastest.
Arguments:
- sent_act: bfloat16 [4, 1024, 4096], P('section', 'groups', 'fsdp'), parts along dimension 1, may hold values from -6 to 6
- sent_grad: bfloat16 [4, 1024, 4096], P('section', 'groups', 'fsdp'), parts along dimension 1, may hold values from -6 to 6
- stash_in: bfloat16 [4, 2, 1024, 4096], P('section', None, 'groups', 'fsdp'), parts along dimension 2, may hold values from -6 to 6
- stash_pre: bfloat16 [4, 2, 1024, 4096], P('section', None, 'groups', 'fsdp'), parts along dimension 2, may hold values from -6 to 6
- layer_weight: bfloat16 [4, 4096, 4096], P('section', None, 'fsdp'), may hold values from -0.125 to 0.125
- layer_bias: float32 [4, 4096], P('section', 'fsdp'), may hold values from -3 to 3
- seg_table: bfloat16 [4784, 4096], P('section', 'fsdp'), may hold values from -6 to 6
- seg_index: int32 [1024, 32], P('groups'), parts along dimension 0, may hold values from 0 to 4783
- seg_amp: float32 [1024, 32], P('groups'), parts along dimension 0, may hold values from -1.2 to 1.2
- field_angle: float32 [1024, 2], P('groups'), parts along dimension 0, may hold values from -1 to 1
- angle_weight: float32 [2, 4096], P(None, 'fsdp'), may hold values from -3 to 3
- target: bfloat16 [1024, 4096], P('groups', 'fsdp'), parts along dimension 0, may hold values from -6 to 6
- sched: int32 [4], P('section'), may hold values from 0 to 1
Outputs:
- fwd_out: bfloat16 [4, 1024, 4096], P('section', 'groups', 'fsdp'), parts along dimension 1
- grad_in: bfloat16 [4, 1024, 4096], P('section', 'groups', 'fsdp'), parts along dimension 1
- grad_w: bfloat16 [4, 8192, 4096], P('section', 'groups', 'fsdp'), parts along dimension 1
- grad_bias: float32 [4, 8192], P('section', ('groups', 'fsdp')), parts along dimension 1
There are 2 independent parts, one for each index of `groups`. A program takes and returns all parts, laid end to end along the dimension named above; an argument that names none is the same for every part. Nothing has to cross between parts.
All inputs are finite; a program needn't handle non-finite values.
Results may differ from a plain program's by a relative error of at most 0.017.
Values may be sent and summed in bfloat16 or wider, within the bound.
A program may use at most 128 MiB of HBM per device.

v0:
```python
import jax
import jax.numpy as jnp
from jax import lax
from jax.sharding import PartitionSpec as P


def from_behind(shard, axis, by):
    length = lax.axis_size(axis)
    pairs = [(i, i + by) for i in range(length) if 0 <= i + by < length]
    return lax.ppermute(shard, axis, pairs)


def lookup_sum(full_table, seg_index, seg_amp, first_row):
    row_count = full_table.shape[0]
    feature_count = full_table.shape[1]
    block_rows = 512
    block_count = (row_count + block_rows - 1) // block_rows
    padded = jnp.pad(full_table, ((0, block_count * block_rows - row_count), (0, 0)))
    blocks = padded.reshape(block_count, block_rows, feature_count)
    starts = jnp.arange(block_count, dtype=jnp.int32) * block_rows
    local_row = seg_index - first_row

    def add_block(total, item):
        table_block, start = item
        position = start + jnp.arange(block_rows, dtype=jnp.int32)
        matched = local_row[:, :, None] == position[None, None, :]
        amplitude = jnp.sum(jnp.where(matched, seg_amp[:, :, None], 0.0), axis=1)
        upper = amplitude.astype(jnp.bfloat16)
        lower = (amplitude - upper.astype(jnp.float32)).astype(jnp.bfloat16)
        total = total + jnp.dot(upper, table_block, preferred_element_type=jnp.float32)
        total = total + jnp.dot(lower, table_block, preferred_element_type=jnp.float32)
        return (total, None)

    empty = jnp.zeros((seg_index.shape[0], feature_count), jnp.float32)
    summed, unused = lax.scan(add_block, empty, (blocks, starts))
    return summed


def local(
    sent_act,
    sent_grad,
    stash_in,
    stash_pre,
    layer_weight,
    layer_bias,
    seg_table,
    seg_index,
    seg_amp,
    field_angle,
    angle_weight,
    target,
    sched,
):
    section_index = lax.axis_index("section")
    section_count = lax.axis_size("section")
    partial_value = lookup_sum(seg_table, seg_index, seg_amp, section_index * seg_table.shape[0])
    embedded = lax.psum(partial_value.astype(jnp.bfloat16), "section").astype(jnp.float32)
    angular = jnp.dot(field_angle, angle_weight, precision=lax.Precision.HIGHEST)
    first_input = (embedded + angular).astype(jnp.bfloat16)
    arrived = from_behind(sent_act[0], "section", 1)
    layer_input = jnp.where(section_index == 0, first_input, arrived)
    from_next = from_behind(sent_grad[0], "section", -1)
    stash_slot = sched[0]
    stashed_in = lax.dynamic_index_in_dim(stash_in[0], stash_slot, 0, keepdims=False)
    stashed_pre = lax.dynamic_index_in_dim(stash_pre[0], stash_slot, 0, keepdims=False)
    stashed_act, pullback = jax.vjp(jax.nn.gelu, stashed_pre.astype(jnp.float32))
    cotangent = jnp.where(
        section_index == section_count - 1,
        stashed_act - target.astype(jnp.float32),
        from_next.astype(jnp.float32),
    )
    pre_grad = pullback(cotangent)[0].astype(jnp.bfloat16)
    grad_bias = jnp.sum(pre_grad.astype(jnp.float32), axis=0)
    weight = layer_weight[0]
    pre_total = jnp.dot(
        lax.all_gather(layer_input, "fsdp", axis=1, tiled=True),
        weight,
        preferred_element_type=jnp.float32,
    )
    grad_total = lax.dot_general(
        lax.all_gather(stashed_in, "fsdp", axis=1, tiled=True),
        pre_grad,
        (((0,), (0,)), ((), ())),
        preferred_element_type=jnp.float32,
    )
    fwd_out = jax.nn.gelu(pre_total + layer_bias[0]).astype(jnp.bfloat16)
    partial_terms = lax.dot_general(
        pre_grad, weight, (((1,), (1,)), ((), ())), preferred_element_type=jnp.float32
    )
    grad_in = lax.psum_scatter(
        partial_terms.astype(jnp.bfloat16), "fsdp", scatter_dimension=1, tiled=True
    )
    return (fwd_out[None], grad_in[None], grad_total.astype(jnp.bfloat16)[None], grad_bias[None])


def solution(mesh):
    return jax.shard_map(
        local,
        mesh=mesh,
        in_specs=(
            P("section", "groups", "fsdp"),
            P("section", "groups", "fsdp"),
            P("section", None, "groups", "fsdp"),
            P("section", None, "groups", "fsdp"),
            P("section", None, "fsdp"),
            P("section", "fsdp"),
            P("section", "fsdp"),
            P("groups", None),
            P("groups", None),
            P("groups", None),
            P(None, "fsdp"),
            P("groups", "fsdp"),
            P("section"),
        ),
        out_specs=(
            P("section", "groups", "fsdp"),
            P("section", "groups", "fsdp"),
            P("section", "groups", "fsdp"),
            P("section", ("groups", "fsdp")),
        ),
        check_vma=False,
    )
```

profile of v0, /device:TPU:0, one launch (start us, length us, event | category | flops | bytes accessed | tf_op | source)
XLA Modules:
  0.0 238.5 jit_solution(12005963658422066757)
XLA Ops:
  8.1 1.1 copy.19
  9.2 1.0 copy.20
  10.2 0.7 broadcast_subtract_fusion
  10.9 3.7 %pad.4 = bf16[1536,1024]{1,0:T(8,128)(2,1)} pad(bf16[1196,1024]{1,0:T(8,128)(2,1)} %param.21, bf16[]{:T(256)} %constant.37.clone.1), padding=0_340x0_0 | pad | bytes 5595138 | tf_op jit(solution)/shard_map/jit(_pad)/pad | solution.py:18
  14.6 53.6 %while.11 = (s32[]{:T(128)}, f32[512,1024]{1,0:T(8,128)}, s32[512,32]{1,0:T(8,128)}, s32[3]{0:T(128)S(1)}, f32[512,32]{1,0:T(8,128)S(1)}, /*index=5*/bf16[3,512,1024]{2,1,0:T(8,128)(2,1)}, s32[]{:T(128)}, s32[]{:T(128)}) while((s32[]{:T(128)}, f32[512,1024]{1,0:T(8,128)}, s32[512,32]{1,0:T(8,128)}, s32[3]{0:T(128)S(1)}, ...), condition=%wide.region_2.3_spmd.clone, body=%wide.region_0.2_spmd.clone.sunk | while | flops 1101529600 | bytes 13766783 | solution.py:35
  15.2 0.6 iota_add_fusion.2
  15.8 9.0 %select_reduce_fusion.2 = f32[512,512]{1,0:T(8,128)S(1)} fusion(f32[512,32]{1,0:T(8,128)S(1)} %get-tuple-element.135, s32[512]{0:T(512)S(1)} %iota_add_fusion.2, s32[512,32]{1,0:T(8,128)} %get-tuple-element.133), kind=kLoop, calls=%fused_computation.clone.1 | loop fusion | flops 24903680 | bytes 1181696 | tf_op jit(solution)/shard_map/while/body/eval_jaxpr/reduce_sum | solution.py:27
  24.8 3.3 %fusion.57 = f32[512,1024]{1,0:T(8,128)} fusion(bf16[3,512,1024]{2,1,0:T(8,128)(2,1)} %get-tuple-element.136, s32[]{:T(128)S(6)} %copy.23, f32[512,512]{1,0:T(8,128)S(1)} %select_reduce_fusion.2), kind=kOutput, calls=%fused_computation.4.clone.1 | convolution fusion | flops 537133056 | bytes 4194308 | tf_op jit(solution)/shard_map/while/body/eval_jaxpr/dot_general | solution.py:30
  28.1 4.0 %fusion.58 = f32[512,1024]{1,0:T(8,128)} fusion(f32[512,1024]{1,0:T(8,128)} %fusion.57, f32[512,1024]{1,0:T(8,128)} %get-tuple-element.124, pred[]{:T(512)S(6)} %compare.4, bf16[3,512,1024]{2,1,0:T(8,128)(2,1)} %get-tuple-element.136, s32[]{:T(128)S(6)} %copy.23, f32[512,512]{1,0:T(8,128)S(1)} %select_reduce_fusion.2), kind=kOutput, calls=%fused_computation.2.clone.1 | convolution fusion | flops 539492352 | bytes 8388613 | tf_op jit(solution)/shard_map/while/body/eval_jaxpr/dot_general | solution.py:31
  32.6 0.6 iota_add_fusion.2
  33.3 9.0 %select_reduce_fusion.2 = f32[512,512]{1,0:T(8,128)S(1)} fusion(f32[512,32]{1,0:T(8,128)S(1)} %get-tuple-element.135, s32[512]{0:T(512)S(1)} %iota_add_fusion.2, s32[512,32]{1,0:T(8,128)} %get-tuple-element.133), kind=kLoop, calls=%fused_computation.clone.1 | loop fusion | flops 24903680 | bytes 1181696 | tf_op jit(solution)/shard_map/while/body/eval_jaxpr/reduce_sum | solution.py:27
  42.3 3.3 %fusion.57 = f32[512,1024]{1,0:T(8,128)} fusion(bf16[3,512,1024]{2,1,0:T(8,128)(2,1)} %get-tuple-element.136, s32[]{:T(128)S(6)} %copy.23, f32[512,512]{1,0:T(8,128)S(1)} %select_reduce_fusion.2), kind=kOutput, calls=%fused_computation.4.clone.1 | convolution fusion | flops 537133056 | bytes 4194308 | tf_op jit(solution)/shard_map/while/body/eval_jaxpr/dot_general | solution.py:30
  45.6 4.6 %fusion.58 = f32[512,1024]{1,0:T(8,128)} fusion(f32[512,1024]{1,0:T(8,128)} %fusion.57, f32[512,1024]{1,0:T(8,128)} %get-tuple-element.124, pred[]{:T(512)S(6)} %compare.4, bf16[3,512,1024]{2,1,0:T(8,128)(2,1)} %get-tuple-element.136, s32[]{:T(128)S(6)} %copy.23, f32[512,512]{1,0:T(8,128)S(1)} %select_reduce_fusion.2), kind=kOutput, calls=%fused_computation.2.clone.1 | convolution fusion | flops 539492352 | bytes 8388613 | tf_op jit(solution)/shard_map/while/body/eval_jaxpr/dot_general | solution.py:31
  50.7 0.6 iota_add_fusion.2
  51.4 9.0 %select_reduce_fusion.2 = f32[512,512]{1,0:T(8,128)S(1)} fusion(f32[512,32]{1,0:T(8,128)S(1)} %get-tuple-element.135, s32[512]{0:T(512)S(1)} %iota_add_fusion.2, s32[512,32]{1,0:T(8,128)} %get-tuple-element.133), kind=kLoop, calls=%fused_computation.clone.1 | loop fusion | flops 24903680 | bytes 1181696 | tf_op jit(solution)/shard_map/while/body/eval_jaxpr/reduce_sum | solution.py:27
  60.4 3.3 %fusion.57 = f32[512,1024]{1,0:T(8,128)} fusion(bf16[3,512,1024]{2,1,0:T(8,128)(2,1)} %get-tuple-element.136, s32[]{:T(128)S(6)} %copy.23, f32[512,512]{1,0:T(8,128)S(1)} %select_reduce_fusion.2), kind=kOutput, calls=%fused_computation.4.clone.1 | convolution fusion | flops 537133056 | bytes 4194308 | tf_op jit(solution)/shard_map/while/body/eval_jaxpr/dot_general | solution.py:30
  63.6 4.6 %fusion.58 = f32[512,1024]{1,0:T(8,128)} fusion(f32[512,1024]{1,0:T(8,128)} %fusion.57, f32[512,1024]{1,0:T(8,128)} %get-tuple-element.124, pred[]{:T(512)S(6)} %compare.4, bf16[3,512,1024]{2,1,0:T(8,128)(2,1)} %get-tuple-element.136, s32[]{:T(128)S(6)} %copy.23, f32[512,512]{1,0:T(8,128)S(1)} %select_reduce_fusion.2), kind=kOutput, calls=%fused_computation.2.clone.1 | convolution fusion | flops 539492352 | bytes 8388613 | tf_op jit(solution)/shard_map/while/body/eval_jaxpr/dot_general | solution.py:31
  68.2 2.7 %convert_element_type.47 = bf16[512,1024]{1,0:T(8,128)(2,1)} convert(f32[512,1024]{1,0:T(8,128)} %get-tuple-element.36) | non-fusion elementwise | flops 524288 | bytes 3145728 | tf_op jit(solution)/shard_map/convert_element_type | solution.py:57
  71.7 1.1 constant_dynamic-slice_fusion
  72.9 5.9 %collective-permute-start = (bf16[512,1024]{1,0:T(8,128)(2,1)}, bf16[512,1024]{1,0:T(8,128)(2,1)}, u32[]{:S(2)}, u32[]{:S(2)}) collective-permute-start(bf16[512,1024]{1,0:T(8,128)(2,1)} %bitcast.1), channel_id=1, source_target_pairs={{0,4},{4,8},{8,12},{1,5},{5,9},{9,13},{2,6},{6,10},{10,14},{3,7},{... | collective-permute-start | bytes 3145736 | tf_op jit(solution)/shard_map/ppermute | solution.py:10
  78.8 38.6 %collective-permute-done = bf16[512,1024]{1,0:T(8,128)(2,1)} collective-permute-done((bf16[512,1024]{1,0:T(8,128)(2,1)}, bf16[512,1024]{1,0:T(8,128)(2,1)}, u32[]{:S(2)}, u32[]{:S(2)}) %collective-permute-start) | collective-permute-done | bytes 1048608 | tf_op jit(solution)/shard_map/ppermute | solution.py:10
  117.4 23.2 %all-reduce.3.cloned.1.call-done = bf16[512,1024]{1,0:T(8,128)(2,1)} async-done(((bf16[512,1024]{1,0:T(8,128)(2,1)}), bf16[512,1024]{1,0:T(8,128)(2,1)}) %all-reduce.3.cloned.1.call-update) | async-done | bytes 1048592 | tf_op jit(solution)/shard_map/psum | solution.py:57
  140.7 4.2 %fusion.42 = bf16[512,1024]{1,0:T(8,128)(2,1)} fusion(bf16[512,1024]{1,0:T(8,128)(2,1)} %collective-permute-done, f32[512,2]{0,1:T(2,128)S(1)} %copy-done.5, f32[2,1024]{1,0:T(2,128)S(1)} %copy-done.4, bf16[512,1024]{1,0:T(8,128)(2,1)} %all-reduce.3.cloned.1.call-done, pred[]{:T(512)S(6)} %eq.19), kind=kOutput, calls=%fused_computation.49 | convolution fusion | flops 14680064 | bytes 3158017 | tf_op jit(solution)/shard_map/dot_general | solution.py:58
  144.9 1.5 collective-permute-start.1
  146.4 25.8 %collective-permute-done.1 = bf16[512,1024]{1,0:T(8,128)(2,1)} collective-permute-done((bf16[512,1024]{1,0:T(8,128)(2,1)}, bf16[512,1024]{1,0:T(8,128)(2,1)}, u32[]{:S(2)}, u32[]{:S(2)}) %collective-permute-start.1) | collective-permute-done | bytes 1048608 | tf_op jit(solution)/shard_map/ppermute | solution.py:10
  172.2 4.1 %convert_reduce_fusion = (f32[1024]{0:T(1024)}, bf16[512,1024]{1,0:T(8,128)(2,1)S(1)}) fusion(bf16[512,1024]{1,0:T(8,128)(2,1)} %collective-permute-done.1, bf16[512,1024]{1,0:T(8,128)(2,1)S(1)} %copy-done.1, bf16[1,2,512,1024]{3,2,1,0:T(8,128)(2,1)} %param.18, s32[]{:T(128)S(6)} %select_n.28, pred[]{:T(512)S(6)} %eq.20), kind=kLoop, calls=%fused_computation.46 | loop fusion | flops 14679040 | bytes 4198405 | tf_op jit(solution)/shard_map/reduce_sum | solution.py:73
  176.3 1.0 copy-done.2
  177.3 9.6 %fusion.14 = bf16[512,4096]{1,0:T(8,128)(2,1)} fusion(bf16[512,1024]{1,0:T(8,128)(2,1)S(1)} %get-tuple-element.77, bf16[1,4096,1024]{2,1,0:T(8,128)(2,1)} %param.19), kind=kOutput, calls=%fused_computation.19 | convolution fusion | flops 4297064448 | bytes 13631488 | tf_op jit(solution)/shard_map/dot_general | solution.py:87
  187.0 1.2 copy-done.3
  188.1 9.0 %convert_bitcast_fusion = bf16[1,4096,1024]{2,1,0:T(8,128)(2,1)} fusion(bf16[512,1024]{1,0:T(8,128)(2,1)S(1)} %copy-done.3, bf16[1,1,512,4096]{3,2,1,0:T(8,128)(2,1)} %all-gather.6.cloned.1.call-done), kind=kOutput, calls=%fused_computation.18 | convolution fusion | flops 4299161600 | bytes 13631488 | tf_op jit(solution)/shard_map/dot_general | solution.py:80
  197.1 10.7 %fusion.39 = bf16[1,512,1024]{2,1,0:T(8,128)(2,1)} fusion(bf16[512,4096]{1,0:T(8,128)(2,1)} %all-gather.4.cloned.1.call-done, bf16[1,4096,1024]{2,1,0:T(8,128)(2,1)} %param.19, f32[1024]{0:T(1024)S(1)} %bitcast.53), kind=kOutput, calls=%fused_computation.48 | convolution fusion | flops 4300210176 | bytes 13635584 | tf_op jit(solution)/shard_map/dot_general | solution.py:75
  207.8 23.1 %reduce-scatter.2.cloned.1.call-done = bf16[512,1024]{1,0:T(8,128)(2,1)} async-done(((bf16[512,4096]{1,0:T(8,128)(2,1)}), bf16[512,1024]{1,0:T(8,128)(2,1)}) %reduce-scatter.2.cloned.1.call-update) | async-done | bytes 1048592 | tf_op jit(solution)/shard_map/reduce_scatter | solution.py:90
  (27 shorter events, 2.0 us)
Async XLA Ops:
  8.0 63.7 %copy-start = (bf16[1,2,512,1024]{3,2,1,0:T(8,128)(2,1)S(1)}, bf16[1,2,512,1024]{3,2,1,0:T(8,128)(2,1)}, u32[]{:S(2)}) copy-start(bf16[1,2,512,1024]{3,2,1,0:T(8,128)(2,1)} %param.17) | copy-start | bytes 6291460
  8.0 132.6 %all-reduce.3.cloned.1.call-start = ((), (), s32[]{:S(2)}) async-start(), calls=%async_computation.1 | async-start | bytes 2097152 | tf_op jit(solution)/shard_map/psum | solution.py:57
  71.0 69.7 %copy-start.4 = (f32[2,1024]{1,0:T(2,128)S(1)}, f32[2,1024]{1,0:T(2,128)}, u32[]{:S(2)}) copy-start(f32[2,1024]{1,0:T(2,128)} %param.25) | copy-start | bytes 24580
  71.0 69.7 %copy-start.5 = (f32[512,2]{0,1:T(2,128)S(1)}, f32[512,2]{0,1:T(2,128)}, u32[]{:S(2)}) copy-start(f32[512,2]{0,1:T(2,128)} %param.24) | copy-start | bytes 12292
  71.0 116.0 %all-gather.6.cloned.1.call-start = ((), (), s32[]{:S(2)}) async-start(), calls=%async_computation.4 | async-start | bytes 5242880 | tf_op jit(solution)/shard_map/all_gather | solution.py:81
  72.9 124.2 %all-gather.4.cloned.1.call-start = ((), (), s32[]{:S(2)}) async-start(), calls=%async_computation.2 | async-start | bytes 5242880 | tf_op jit(solution)/shard_map/all_gather | solution.py:76
  72.9 44.5 %collective-permute-start = (bf16[512,1024]{1,0:T(8,128)(2,1)}, bf16[512,1024]{1,0:T(8,128)(2,1)}, u32[]{:S(2)}, u32[]{:S(2)}) collective-permute-start(bf16[512,1024]{1,0:T(8,128)(2,1)} %bitcast.1), channel_id=1, source_target_pairs={{0,4},{4,8},{8,12},{1,5},{5,9},{9,13},{2,6},{6,10},{10,14},{3,7},{... | collective-permute-start | bytes 3145736 | tf_op jit(solution)/shard_map/ppermute | solution.py:10
  78.8 93.4 %copy-start.1 = (bf16[512,1024]{1,0:T(8,128)(2,1)S(1)}, bf16[512,1024]{1,0:T(8,128)(2,1)}, u32[]{:S(2)}) copy-start(bf16[512,1024]{1,0:T(8,128)(2,1)} %param.26) | copy-start | bytes 3145732
  144.9 86.0 %reduce-scatter.2.cloned.1.call-start = ((), (), s32[]{:S(2)}) async-start(), calls=%async_computation.3 | async-start | bytes 5242880 | tf_op jit(solution)/shard_map/reduce_scatter | solution.py:90
  144.9 27.3 %collective-permute-start.1 = (bf16[512,1024]{1,0:T(8,128)(2,1)}, bf16[512,1024]{1,0:T(8,128)(2,1)}, u32[]{:S(2)}, u32[]{:S(2)}) collective-permute-start(bf16[512,1024]{1,0:T(8,128)(2,1)} %bitcast.51), channel_id=1, source_target_pairs={{4,0},{8,4},{12,8},{5,1},{9,5},{13,9},{6,2},{10,6},{14,10},{7,3},{... | collective-permute-start | bytes 3145736 | tf_op jit(solution)/shard_map/ppermute | solution.py:10
  176.3 1.0 copy-start.2
  186.9 1.2 copy-start.3
  186.9 10.2 %copy-start.6 = (f32[1,1024]{1,0:T(1,128)S(1)}, f32[1,1024]{1,0:T(1,128)}, u32[]{:S(2)}) copy-start(f32[1,1024]{1,0:T(1,128)} %param.20) | copy-start | bytes 12292
Sparse Core Ops, SparseCore 0:
  71.1 69.4 all-reduce.2
Sparse Core Ops, SparseCore 1:
  73.0 37.0 all-gather.5
  144.9 34.0 all-gather.3
  187.0 43.8 reduce-scatter.1
where the time goes:
time: 239 us; the launch traced here: 238 us
  waiting for transfers between devices  111 us (46%)
  matrix products  56.4 us (24%)
  other arithmetic  36.4 us (15%)
  between operations  16.4 us (7%)
  local copies, waits for them, and re-layouts  10.8 us (5%)
  starting transfers between devices  7.57 us (3%)
    ppermute x2, waiting for transfers between devices, from_behind(): return lax.ppermute(shard, axis, pairs)  64.4 us
    reduce_sum x3, other arithmetic, add_block(): amplitude = jnp.sum(jnp.where(matched, seg_amp[:, :, None], 0.0), axis=1)  26.9 us
    psum x1, waiting for transfers between devices, local(): lax.psum(partial_value.astype(jnp.bfloat16), 'section').astype(jnp.float32)  23.2 us
    reduce_scatter x1, waiting for transfers between devices, local(): lax.psum_scatter(partial_terms.astype(jnp.bfloat16), 'fsdp', scatter_dime...  23.1 us
    dot_general x3, matrix products, add_block(): jnp.dot(lower, table_block, preferred_element_type=jnp.float32)  13.2 us
    dot_general x1, matrix products, local(): jnp.dot(lax.all_gather(layer_input, 'fsdp', axis=1, tiled=True), weight,...  10.7 us
    dot_general x3, matrix products, add_block(): jnp.dot(upper, table_block, preferred_element_type=jnp.float32)  9.82 us
    dot_general x1, matrix products, local(): lax.dot_general(pre_grad, weight, (((1,), (1,)), ((), ())), preferred_ele...  9.61 us
  transfers between devices with their start and end apart: 6, of which 4 were waited for; matrix products, arithmetic and copies ran while one was open for 16% of the time, Pallas kernels for 0%

commit v1 on v0

--- a/solution.py
+++ b/solution.py
@@ -54,7 +54,12 @@
     section_index = lax.axis_index("section")
     section_count = lax.axis_size("section")
     partial_value = lookup_sum(seg_table, seg_index, seg_amp, section_index * seg_table.shape[0])
-    embedded = lax.psum(partial_value.astype(jnp.bfloat16), "section").astype(jnp.float32)
+
+    def note_ladders_over_axis(incoming_x):
+        field_out = jnp.sum(lax.all_gather(incoming_x, "section"), axis=0)
+        return field_out
+
+    embedded = note_ladders_over_axis(partial_value.astype(jnp.bfloat16)).astype(jnp.float32)
     angular = jnp.dot(field_angle, angle_weight, precision=lax.Precision.HIGHEST)
     first_input = (embedded + angular).astype(jnp.bfloat16)
     arrived = from_behind(sent_act[0], "section", 1)

time: 239 us -> 298 us (1.25)
  waiting for transfers between devices: 111 us -> 171 us
  other arithmetic: 36.4 us -> 40 us
    all_gather x0 -> x1, waiting for transfers between devices: none -> 89.4 us  [note_ladders_over_axis(): field_out = jnp.sum(lax.all_gather(incoming_x, 'section'), axis=0)]
    ppermute x2, waiting for transfers between devices: 64.4 us -> 28 us  [from_behind(): return lax.ppermute(shard, axis, pairs)]
    psum x1 -> x0, waiting for transfers between devices: 23.2 us -> none  [local(): lax.psum(partial_value.astype(jnp.bfloat16), 'section').astype(jnp.float32)]
    all_gather x1, waiting for transfers between devices: 0.01 us -> 16.4 us  [local(): lax.all_gather(layer_input, 'fsdp', axis=1, tiled=True)]
    reduce_scatter x1, waiting for transfers between devices: 23.1 us -> 36.9 us  [local(): lax.psum_scatter(partial_terms.astype(jnp.bfloat16), 'fsdp', scatter_dime...]
    reduce_sum x0 -> x1, other arithmetic: none -> 3.35 us  [note_ladders_over_axis(): field_out = jnp.sum(lax.all_gather(incoming_x, 'section'), axis=0)]
  transfers between devices with their start and end apart: 6 -> 6, of which waited for: 4 -> 4; matrix products, arithmetic and copies ran while one was open for 16% -> 14% of each run, Pallas kernels for 0% -> 0%
where the time goes in v1:
time: 298 us; the launch traced here: 297 us
  waiting for transfers between devices  171 us (57%)
  matrix products  55.1 us (18%)
  other arithmetic  40 us (13%)
  between operations  14.5 us (5%)
  local copies, waits for them, and re-layouts  8.59 us (3%)
  starting transfers between devices  7.63 us (3%)
    all_gather x1, waiting for transfers between devices, note_ladders_over_axis(): field_out = jnp.sum(lax.all_gather(incoming_x, 'section'), axis=0)  89.4 us
    reduce_scatter x1, waiting for transfers between devices, local(): lax.psum_scatter(partial_terms.astype(jnp.bfloat16), 'fsdp', scatter_dime...  36.9 us
    ppermute x2, waiting for transfers between devices, from_behind(): return lax.ppermute(shard, axis, pairs)  28 us
    reduce_sum x3, other arithmetic, add_block(): amplitude = jnp.sum(jnp.where(matched, seg_amp[:, :, None], 0.0), axis=1)  26.9 us
    all_gather x1, waiting for transfers between devices, local(): lax.all_gather(layer_input, 'fsdp', axis=1, tiled=True)  16.4 us
    dot_general x3, matrix products, add_block(): jnp.dot(lower, table_block, preferred_element_type=jnp.float32)  13.1 us
    dot_general x1, matrix products, local(): jnp.dot(lax.all_gather(layer_input, 'fsdp', axis=1, tiled=True), weight,...  10.6 us
    dot_general x3, matrix products, add_block(): jnp.dot(upper, table_block, preferred_element_type=jnp.float32)  9.87 us
  transfers between devices with their start and end apart: 6, of which 4 were waited for; matrix products, arithmetic and copies ran while one was open for 14% of the time, Pallas kernels for 0%

profile of v1, /device:TPU:0, one launch (start us, length us, event | category | flops | bytes accessed | tf_op | source)
XLA Modules:
  0.0 296.8 jit_solution(17201320122542406387)
XLA Ops:
  7.2 1.1 copy.19
  8.4 1.0 copy.20
  9.3 0.7 broadcast_subtract_fusion
  10.1 3.7 %pad.4 = bf16[1536,1024]{1,0:T(8,128)(2,1)} pad(bf16[1196,1024]{1,0:T(8,128)(2,1)} %param.21, bf16[]{:T(256)} %constant.38.clone.1), padding=0_340x0_0 | pad | bytes 5595138 | tf_op jit(solution)/shard_map/jit(_pad)/pad | solution.py:18
  13.8 53.6 %while.11 = (s32[]{:T(128)}, f32[512,1024]{1,0:T(8,128)}, s32[512,32]{1,0:T(8,128)}, s32[3]{0:T(128)S(1)}, f32[512,32]{1,0:T(8,128)S(1)}, /*index=5*/bf16[3,512,1024]{2,1,0:T(8,128)(2,1)}, s32[]{:T(128)}, s32[]{:T(128)}) while((s32[]{:T(128)}, f32[512,1024]{1,0:T(8,128)}, s32[512,32]{1,0:T(8,128)}, s32[3]{0:T(128)S(1)}, ...), condition=%wide.region_2.3_spmd.clone, body=%wide.region_0.2_spmd.clone.sunk | while | flops 1101529600 | bytes 13766783 | solution.py:35
  14.4 0.6 iota_add_fusion.2
  15.0 9.0 %select_reduce_fusion.2 = f32[512,512]{1,0:T(8,128)S(1)} fusion(f32[512,32]{1,0:T(8,128)S(1)} %get-tuple-element.135, s32[512]{0:T(512)S(1)} %iota_add_fusion.2, s32[512,32]{1,0:T(8,128)} %get-tuple-element.133), kind=kLoop, calls=%fused_computation.clone.1 | loop fusion | flops 24903680 | bytes 1181696 | tf_op jit(solution)/shard_map/while/body/eval_jaxpr/reduce_sum | solution.py:27
  24.0 3.3 %fusion.57 = f32[512,1024]{1,0:T(8,128)} fusion(bf16[3,512,1024]{2,1,0:T(8,128)(2,1)} %get-tuple-element.136, s32[]{:T(128)S(6)} %copy.23, f32[512,512]{1,0:T(8,128)S(1)} %select_reduce_fusion.2), kind=kOutput, calls=%fused_computation.4.clone.1 | convolution fusion | flops 537133056 | bytes 4194308 | tf_op jit(solution)/shard_map/while/body/eval_jaxpr/dot_general | solution.py:30
  27.3 3.9 %fusion.58 = f32[512,1024]{1,0:T(8,128)} fusion(f32[512,1024]{1,0:T(8,128)} %fusion.57, f32[512,1024]{1,0:T(8,128)} %get-tuple-element.124, pred[]{:T(512)S(6)} %compare.4, bf16[3,512,1024]{2,1,0:T(8,128)(2,1)} %get-tuple-element.136, s32[]{:T(128)S(6)} %copy.23, f32[512,512]{1,0:T(8,128)S(1)} %select_reduce_fusion.2), kind=kOutput, calls=%fused_computation.2.clone.1 | convolution fusion | flops 539492352 | bytes 8388613 | tf_op jit(solution)/shard_map/while/body/eval_jaxpr/dot_general | solution.py:31
  31.2 0.6 dynamic_slice.35
  31.8 0.6 iota_add_fusion.2
  32.5 9.0 %select_reduce_fusion.2 = f32[512,512]{1,0:T(8,128)S(1)} fusion(f32[512,32]{1,0:T(8,128)S(1)} %get-tuple-element.135, s32[512]{0:T(512)S(1)} %iota_add_fusion.2, s32[512,32]{1,0:T(8,128)} %get-tuple-element.133), kind=kLoop, calls=%fused_computation.clone.1 | loop fusion | flops 24903680 | bytes 1181696 | tf_op jit(solution)/shard_map/while/body/eval_jaxpr/reduce_sum | solution.py:27
  41.4 3.3 %fusion.57 = f32[512,1024]{1,0:T(8,128)} fusion(bf16[3,512,1024]{2,1,0:T(8,128)(2,1)} %get-tuple-element.136, s32[]{:T(128)S(6)} %copy.23, f32[512,512]{1,0:T(8,128)S(1)} %select_reduce_fusion.2), kind=kOutput, calls=%fused_computation.4.clone.1 | convolution fusion | flops 537133056 | bytes 4194308 | tf_op jit(solution)/shard_map/while/body/eval_jaxpr/dot_general | solution.py:30
  44.7 4.6 %fusion.58 = f32[512,1024]{1,0:T(8,128)} fusion(f32[512,1024]{1,0:T(8,128)} %fusion.57, f32[512,1024]{1,0:T(8,128)} %get-tuple-element.124, pred[]{:T(512)S(6)} %compare.4, bf16[3,512,1024]{2,1,0:T(8,128)(2,1)} %get-tuple-element.136, s32[]{:T(128)S(6)} %copy.23, f32[512,512]{1,0:T(8,128)S(1)} %select_reduce_fusion.2), kind=kOutput, calls=%fused_computation.2.clone.1 | convolution fusion | flops 539492352 | bytes 8388613 | tf_op jit(solution)/shard_map/while/body/eval_jaxpr/dot_general | solution.py:31
  49.9 0.6 iota_add_fusion.2
  50.6 9.0 %select_reduce_fusion.2 = f32[512,512]{1,0:T(8,128)S(1)} fusion(f32[512,32]{1,0:T(8,128)S(1)} %get-tuple-element.135, s32[512]{0:T(512)S(1)} %iota_add_fusion.2, s32[512,32]{1,0:T(8,128)} %get-tuple-element.133), kind=kLoop, calls=%fused_computation.clone.1 | loop fusion | flops 24903680 | bytes 1181696 | tf_op jit(solution)/shard_map/while/body/eval_jaxpr/reduce_sum | solution.py:27
  59.5 3.3 %fusion.57 = f32[512,1024]{1,0:T(8,128)} fusion(bf16[3,512,1024]{2,1,0:T(8,128)(2,1)} %get-tuple-element.136, s32[]{:T(128)S(6)} %copy.23, f32[512,512]{1,0:T(8,128)S(1)} %select_reduce_fusion.2), kind=kOutput, calls=%fused_computation.4.clone.1 | convolution fusion | flops 537133056 | bytes 4194308 | tf_op jit(solution)/shard_map/while/body/eval_jaxpr/dot_general | solution.py:30
  62.8 4.6 %fusion.58 = f32[512,1024]{1,0:T(8,128)} fusion(f32[512,1024]{1,0:T(8,128)} %fusion.57, f32[512,1024]{1,0:T(8,128)} %get-tuple-element.124, pred[]{:T(512)S(6)} %compare.4, bf16[3,512,1024]{2,1,0:T(8,128)(2,1)} %get-tuple-element.136, s32[]{:T(128)S(6)} %copy.23, f32[512,512]{1,0:T(8,128)S(1)} %select_reduce_fusion.2), kind=kOutput, calls=%fused_computation.2.clone.1 | convolution fusion | flops 539492352 | bytes 8388613 | tf_op jit(solution)/shard_map/while/body/eval_jaxpr/dot_general | solution.py:31
  67.4 2.7 convert_element_type.49
  70.9 1.0 constant_dynamic-slice_fusion
  72.0 6.0 %collective-permute-start = (bf16[512,1024]{1,0:T(8,128)(2,1)}, bf16[512,1024]{1,0:T(8,128)(2,1)}, u32[]{:S(2)}, u32[]{:S(2)}) collective-permute-start(bf16[512,1024]{1,0:T(8,128)(2,1)} %bitcast.2), channel_id=1, source_target_pairs={{0,4},{4,8},{8,12},{1,5},{5,9},{9,13},{2,6},{6,10},{10,14},{3,7},{... | collective-permute-start | bytes 3145736 | tf_op jit(solution)/shard_map/ppermute | solution.py:10
  78.0 89.4 %all-gather.8.cloned.1.call-done = bf16[2048,1024]{1,0:T(8,128)(2,1)} async-done(((bf16[512,1024]{1,0:T(8,128)(2,1)}), bf16[2048,1024]{1,0:T(8,128)(2,1)}) %all-gather.8.cloned.1.call-update) | async-done | bytes 4194320 | tf_op jit(solution)/shard_map/all_gather | solution.py:59
  167.4 3.3 %reduce_sum.30 = bf16[512,1024]{1,0:T(8,128)(2,1)S(1)} reduce(bf16[4,512,1024]{2,1,0:T(8,128)(2,1)} %bitcast.51, bf16[]{:T(256)} %constant.38.clone.1), dimensions={0}, to_apply=%region_3.4 | reduce | flops 1572864 | bytes 5242882 | tf_op jit(solution)/shard_map/reduce_sum | solution.py:59
  170.8 3.0 %fusion.42 = bf16[512,1024]{1,0:T(8,128)(2,1)} fusion(bf16[512,1024]{1,0:T(8,128)(2,1)} %collective-permute-done, f32[512,2]{0,1:T(2,128)S(1)} %copy-done.2, f32[2,1024]{1,0:T(2,128)S(1)} %copy-done.1, bf16[512,1024]{1,0:T(8,128)(2,1)S(1)} %reduce_sum.30, pred[]{:T(512)S(6)} %eq.19), kind=kOutput, calls=%fused_computation.49 | convolution fusion | flops 14680064 | bytes 3158017 | tf_op jit(solution)/shard_map/dot_general | solution.py:63
  173.9 1.5 collective-permute-start.1
  175.4 28.0 %collective-permute-done.1 = bf16[512,1024]{1,0:T(8,128)(2,1)} collective-permute-done((bf16[512,1024]{1,0:T(8,128)(2,1)}, bf16[512,1024]{1,0:T(8,128)(2,1)}, u32[]{:S(2)}, u32[]{:S(2)}) %collective-permute-start.1) | collective-permute-done | bytes 1048608 | tf_op jit(solution)/shard_map/ppermute | solution.py:10
  203.4 4.3 %convert_reduce_fusion = (f32[1024]{0:T(1024)}, bf16[512,1024]{1,0:T(8,128)(2,1)S(1)}) fusion(bf16[512,1024]{1,0:T(8,128)(2,1)} %collective-permute-done.1, bf16[512,1024]{1,0:T(8,128)(2,1)} %param.26, bf16[1,2,512,1024]{3,2,1,0:T(8,128)(2,1)} %param.18, s32[]{:T(128)S(6)} %select_n.28, pred[]{:T(512)S(6)} %eq.20), kind=kLoop, calls=%fused_computation.46 | loop fusion | flops 14679040 | bytes 4198405 | tf_op jit(solution)/shard_map/reduce_sum | solution.py:78
  207.7 9.5 %fusion.14 = bf16[512,4096]{1,0:T(8,128)(2,1)} fusion(bf16[512,1024]{1,0:T(8,128)(2,1)S(1)} %get-tuple-element.77, bf16[1,4096,1024]{2,1,0:T(8,128)(2,1)} %param.19), kind=kOutput, calls=%fused_computation.19 | convolution fusion | flops 4297064448 | bytes 13631488 | tf_op jit(solution)/shard_map/dot_general | solution.py:92
  217.3 9.1 %convert_bitcast_fusion = bf16[1,4096,1024]{2,1,0:T(8,128)(2,1)} fusion(bf16[512,1024]{1,0:T(8,128)(2,1)S(1)} %get-tuple-element.77, bf16[1,1,512,4096]{3,2,1,0:T(8,128)(2,1)} %all-gather.10.cloned.1.call-done), kind=kOutput, calls=%fused_computation.18 | convolution fusion | flops 4299161600 | bytes 13631488 | tf_op jit(solution)/shard_map/dot_general | solution.py:85
  226.4 16.4 %all-gather.6.cloned.1.call-done = bf16[512,4096]{1,0:T(8,128)(2,1)} async-done(((bf16[512,1024]{1,0:T(8,128)(2,1)}), bf16[512,4096]{1,0:T(8,128)(2,1)}) %all-gather.6.cloned.1.call-update) | async-done | bytes 4194320 | tf_op jit(solution)/shard_map/all_gather | solution.py:81
  242.8 10.6 %fusion.39 = bf16[1,512,1024]{2,1,0:T(8,128)(2,1)} fusion(bf16[512,4096]{1,0:T(8,128)(2,1)} %all-gather.6.cloned.1.call-done, bf16[1,4096,1024]{2,1,0:T(8,128)(2,1)} %param.19, f32[1024]{0:T(1024)S(1)} %bitcast.55), kind=kOutput, calls=%fused_computation.48 | convolution fusion | flops 4300210176 | bytes 13635584 | tf_op jit(solution)/shard_map/dot_general | solution.py:80
  253.4 36.9 %reduce-scatter.2.cloned.1.call-done = bf16[512,1024]{1,0:T(8,128)(2,1)} async-done(((bf16[512,4096]{1,0:T(8,128)(2,1)}), bf16[512,1024]{1,0:T(8,128)(2,1)}) %reduce-scatter.2.cloned.1.call-update) | async-done | bytes 1048592 | tf_op jit(solution)/shard_map/reduce_scatter | solution.py:95
  (22 shorter events, 1.4 us)
Async XLA Ops:
  7.2 63.7 %copy-start = (bf16[1,2,512,1024]{3,2,1,0:T(8,128)(2,1)S(1)}, bf16[1,2,512,1024]{3,2,1,0:T(8,128)(2,1)}, u32[]{:S(2)}) copy-start(bf16[1,2,512,1024]{3,2,1,0:T(8,128)(2,1)} %param.17) | copy-start | bytes 6291460
  7.2 160.3 %all-gather.8.cloned.1.call-start = ((), (), s32[]{:S(2)}) async-start(), calls=%async_computation.3 | async-start | bytes 5242880 | tf_op jit(solution)/shard_map/all_gather | solution.py:59
  70.2 147.1 %all-gather.10.cloned.1.call-start = ((), (), s32[]{:S(2)}) async-start(), calls=%async_computation.4 | async-start | bytes 5242880 | tf_op jit(solution)/shard_map/all_gather | solution.py:86
  71.9 170.9 %all-gather.6.cloned.1.call-start = ((), (), s32[]{:S(2)}) async-start(), calls=%async_computation.1 | async-start | bytes 5242880 | tf_op jit(solution)/shard_map/all_gather | solution.py:81
  72.0 98.8 %collective-permute-start = (bf16[512,1024]{1,0:T(8,128)(2,1)}, bf16[512,1024]{1,0:T(8,128)(2,1)}, u32[]{:S(2)}, u32[]{:S(2)}) collective-permute-start(bf16[512,1024]{1,0:T(8,128)(2,1)} %bitcast.2), channel_id=1, source_target_pairs={{0,4},{4,8},{8,12},{1,5},{5,9},{9,13},{2,6},{6,10},{10,14},{3,7},{... | collective-permute-start | bytes 3145736 | tf_op jit(solution)/shard_map/ppermute | solution.py:10
  167.4 3.4 %copy-start.1 = (f32[2,1024]{1,0:T(2,128)S(1)}, f32[2,1024]{1,0:T(2,128)}, u32[]{:S(2)}) copy-start(f32[2,1024]{1,0:T(2,128)} %param.25) | copy-start | bytes 24580
  167.4 3.4 %copy-start.2 = (f32[512,2]{0,1:T(2,128)S(1)}, f32[512,2]{0,1:T(2,128)}, u32[]{:S(2)}) copy-start(f32[512,2]{0,1:T(2,128)} %param.24) | copy-start | bytes 12292
  173.8 116.5 %reduce-scatter.2.cloned.1.call-start = ((), (), s32[]{:S(2)}) async-start(), calls=%async_computation.2 | async-start | bytes 5242880 | tf_op jit(solution)/shard_map/reduce_scatter | solution.py:95
  173.9 29.5 %collective-permute-start.1 = (bf16[512,1024]{1,0:T(8,128)(2,1)}, bf16[512,1024]{1,0:T(8,128)(2,1)}, u32[]{:S(2)}, u32[]{:S(2)}) collective-permute-start(bf16[512,1024]{1,0:T(8,128)(2,1)} %bitcast.53), channel_id=1, source_target_pairs={{4,0},{8,4},{12,8},{5,1},{9,5},{13,9},{6,2},{10,6},{14,10},{7,3},{... | collective-permute-start | bytes 3145736 | tf_op jit(solution)/shard_map/ppermute | solution.py:10
  217.2 25.6 %copy-start.3 = (f32[1,1024]{1,0:T(1,128)S(1)}, f32[1,1024]{1,0:T(1,128)}, u32[]{:S(2)}) copy-start(f32[1,1024]{1,0:T(1,128)} %param.20) | copy-start | bytes 12292
Sparse Core Ops, SparseCore 0:
  70.3 97.1 all-gather.7
  169.6 36.5 all-gather.9
  208.3 34.4 all-gather.5
  245.8 44.4 reduce-scatter.1
